TPU v7x, 32 devices: a whole 2x2x4 slice. The times are simulated.
32 devices in a mesh: groups: 2 (over x), loop: 4 (over y, core), bulk: 4 (over z).
Axes of the slice: x: 2, y: 2, z: 4, core: 2. Of those that a mesh axis runs over, the one named last changes fastest.
Arguments:
- tokens: bfloat16 [512, 8192], P(('groups', 'bulk'), 'loop'), parts along dimension 0, may hold values from -6 to 6
- gate_weight: bfloat16 [8192, 26624], P('loop', 'bulk'), may hold values from -0.0625 to 0.0625
- up_weight: bfloat16 [8192, 26624], P('loop', 'bulk'), may hold values from -0.0625 to 0.0625
- down_weight: bfloat16 [26624, 8192], P('bulk', 'loop'), may hold values from -0.0390625 to 0.0390625
Outputs:
- mixed: bfloat16 [512, 8192], P(('groups', 'bulk'), 'loop'), parts along dimension 0
There are 2 independent parts, one for each index of `groups`. A program takes and returns all parts, laid end to end along the dimension named above; an argument that names none is the same for every part. Nothing has to cross between parts.
All inputs are finite; a program needn't handle non-finite values.
Results may differ from a plain program's by a relative error of at most 0.019.
Values may be sent and summed in bfloat16 or wider, within the bound.
A program may use at most 192 MiB of HBM per device.

v0:
```python
import jax
import jax.numpy as jnp
from jax import lax
from jax.sharding import PartitionSpec as P


def body(tokens, gate_weight, up_weight, down_weight):
    hidden_cols = gate_weight.shape[1]
    piece = lax.all_gather(tokens, "bulk", axis=0, tiled=True)
    gate_piece = jnp.dot(piece, gate_weight, preferred_element_type=jnp.float32)
    up_piece = jnp.dot(piece, up_weight, preferred_element_type=jnp.float32)
    partial_sums = jnp.concatenate([gate_piece, up_piece], axis=1)
    summed = lax.psum_scatter(
        partial_sums.astype(jnp.bfloat16), "loop", scatter_dimension=0, tiled=True
    ).astype(jnp.float32)
    hidden = (jax.nn.silu(summed[:, :hidden_cols]) * summed[:, hidden_cols:]).astype(jnp.bfloat16)
    terms = jnp.dot(
        lax.all_gather(hidden, "loop", axis=0, tiled=True),
        down_weight,
        preferred_element_type=jnp.float32,
    )
    result = lax.psum_scatter(terms.astype(jnp.bfloat16), "bulk", scatter_dimension=0, tiled=True)
    return result


def solution(mesh):
    return jax.shard_map(
        body,
        mesh=mesh,
        in_specs=(
            P(("groups", "bulk"), "loop"),
            P("loop", "bulk"),
            P("loop", "bulk"),
            P("bulk", "loop"),
        ),
        out_specs=P(("groups", "bulk"), "loop"),
        check_vma=False,
    )
```

profile of v0, /device:TPU:0, one launch (start us, length us, event | category | flops | bytes accessed | tf_op | source)
XLA Modules:
  0.0 215.0 jit_solution(1009295030296564351)
XLA Ops:
  6.5 0.0 all-gather.3.cloned.1.call-start
  6.5 0.7 all-gather.3.cloned.1.call-update
  7.3 0.0 reduce-scatter.3.cloned.1.call-start
  7.3 32.3 %all-gather.3.cloned.1.call-done = bf16[256,2048]{1,0:T(8,128)(2,1)} async-done(((bf16[64,2048]{1,0:T(8,128)(2,1)}), bf16[256,2048]{1,0:T(8,128)(2,1)}) %all-gather.3.cloned.1.call-update) | async-done | bytes 1048592 | tf_op jit(solution)/shard_map/all_gather | solution.py:9
  39.6 0.0 copy-start
  39.6 16.4 %convolution_convert_fusion = bf16[256,6656]{1,0:T(8,128)(2,1)S(1)} fusion(bf16[256,2048]{1,0:T(8,128)(2,1)} %all-gather.3.cloned.1.call-done, bf16[2048,6656]{1,0:T(8,128)(2,1)} %param.6), kind=kOutput, calls=%fused_computation | convolution fusion | flops 6981025792 | bytes 31719424 | tf_op jit(solution)/shard_map/dot_general | solution.py:11
  56.0 0.0 copy-done
  56.0 12.5 %convolution_convert_fusion.1 = bf16[256,6656]{1,0:T(8,128)(2,1)S(1)} fusion(bf16[256,2048]{1,0:T(8,128)(2,1)S(1)} %copy-done, bf16[2048,6656]{1,0:T(8,128)(2,1)} %param.5), kind=kOutput, calls=%fused_computation.1 | convolution fusion | flops 6981025792 | bytes 31719424 | tf_op jit(solution)/shard_map/dot_general | solution.py:10
  68.4 3.7 %pad_maximum_fusion = bf16[256,13312]{1,0:T(8,128)(2,1)} fusion(bf16[256,6656]{1,0:T(8,128)(2,1)S(1)} %convolution_convert_fusion, bf16[256,6656]{1,0:T(8,128)(2,1)S(1)} %convolution_convert_fusion.1), kind=kLoop, calls=%fused_computation.2 | loop fusion | flops 13631488 | bytes 13631488 | tf_op jit(solution)/shard_map/concatenate | solution.py:12
  72.1 0.0 reduce-scatter.3.cloned.1.call-update
  72.2 0.0 all-gather.5.cloned.1.call-start
  72.2 61.5 %reduce-scatter.3.cloned.1.call-done = bf16[64,13312]{1,0:T(8,128)(2,1)} async-done(((bf16[256,13312]{1,0:T(8,128)(2,1)}), bf16[64,13312]{1,0:T(8,128)(2,1)}) %reduce-scatter.3.cloned.1.call-update) | async-done | bytes 1703952 | tf_op jit(solution)/shard_map/reduce_scatter | solution.py:13
  133.7 1.7 convert_element_type.10
  135.3 1.4 fusion
  136.7 0.0 all-gather.5.cloned.1.call-update
  136.7 0.0 reduce-scatter.5.cloned.1.call-start
  136.8 30.1 %all-gather.5.cloned.1.call-done = bf16[256,6656]{1,0:T(8,128)(2,1)} async-done(((bf16[64,6656]{1,0:T(8,128)(2,1)}), bf16[256,6656]{1,0:T(8,128)(2,1)}) %all-gather.5.cloned.1.call-update) | async-done | bytes 3407888 | tf_op jit(solution)/shard_map/all_gather | solution.py:18
  166.9 14.2 %convolution_convert_fusion.2 = bf16[256,2048]{1,0:T(8,128)(2,1)} fusion(bf16[256,6656]{1,0:T(8,128)(2,1)} %all-gather.5.cloned.1.call-done, bf16[6656,2048]{1,0:T(8,128)(2,1)} %param.7), kind=kOutput, calls=%fused_computation.3 | convolution fusion | flops 6979846144 | bytes 31719424 | tf_op jit(solution)/shard_map/dot_general | solution.py:17
  181.2 0.0 reduce-scatter.5.cloned.1.call-update
  181.2 27.3 %reduce-scatter.5.cloned.1.call-done = bf16[64,2048]{1,0:T(8,128)(2,1)} async-done(((bf16[256,2048]{1,0:T(8,128)(2,1)}), bf16[64,2048]{1,0:T(8,128)(2,1)}) %reduce-scatter.5.cloned.1.call-update) | async-done | bytes 262160 | tf_op jit(solution)/shard_map/reduce_scatter | solution.py:22
Async XLA Ops:
  6.5 33.1 %all-gather.3.cloned.1.call-start = ((), (), s32[]{:S(2)}) async-start(), calls=%async_computation.2 | async-start | bytes 1310720 | tf_op jit(solution)/shard_map/all_gather | solution.py:9
  7.3 126.4 %reduce-scatter.3.cloned.1.call-start = ((), (), s32[]{:S(2)}) async-start(), calls=%async_computation.3 | async-start | bytes 8519680 | tf_op jit(solution)/shard_map/reduce_scatter | solution.py:13
  39.6 16.4 %copy-start = (bf16[256,2048]{1,0:T(8,128)(2,1)S(1)}, bf16[256,2048]{1,0:T(8,128)(2,1)}, u32[]{:S(2)}) copy-start(bf16[256,2048]{1,0:T(8,128)(2,1)} %all-gather.3.cloned.1.call-done) | copy-start | bytes 3145732
  72.2 94.8 %all-gather.5.cloned.1.call-start = ((), (), s32[]{:S(2)}) async-start(), calls=%async_computation.4 | async-start | bytes 4259840 | tf_op jit(solution)/shard_map/all_gather | solution.py:18
  136.7 71.7 %reduce-scatter.5.cloned.1.call-start = ((), (), s32[]{:S(2)}) async-start(), calls=%async_computation.5 | async-start | bytes 1310720 | tf_op jit(solution)/shard_map/reduce_scatter | solution.py:22
Sparse Core Ops, SparseCore 0:
  8.9 30.6 all-gather.2
  72.3 61.3 reduce-scatter.2
  136.9 30.0 all-gather.4
  181.3 27.1 reduce-scatter.4
where the time goes:
time: 215 us
  waiting for transfers between devices  152 us (71%)
  matrix products  43.1 us (20%)
  between operations  13.2 us (6%)
  other arithmetic  6.73 us (3%)
    reduce_scatter x1, waiting for transfers between devices, body(): lax.psum_scatter(partial_sums.astype(jnp.bfloat16), 'loop', scatter_dimen...  61.5 us
    all_gather x1, waiting for transfers between devices, body(): piece = lax.all_gather(tokens, 'bulk', axis=0, tiled=True)  32.3 us
    all_gather x1, waiting for transfers between devices, body(): lax.all_gather(hidden, 'loop', axis=0, tiled=True)  30.1 us
    reduce_scatter x1, waiting for transfers between devices, body(): lax.psum_scatter(terms.astype(jnp.bfloat16), 'bulk', scatter_dimension=0,...  27.3 us
    dot_general x1, matrix products, body(): up_piece = jnp.dot(piece, up_weight, preferred_element_type=jnp.float32)  16.4 us
    dot_general x1, matrix products, body(): jnp.dot(lax.all_gather(hidden, 'loop', axis=0, tiled=True), down_weight,...  14.2 us
    dot_general x1, matrix products, body(): gate_piece = jnp.dot(piece, gate_weight, preferred_element_type=jnp.float32)  12.5 us
  transfers between devices with their start and end apart: 4, of which 4 were waited for; matrix products, arithmetic and copies ran while one was open for 0% of the time, Pallas kernels for 0%

commit v1 on v0

v1 whole, which is shorter than its diff:
```python
import functools

import jax
import jax.numpy as jnp
from jax import lax
from jax.experimental import pallas as pl
from jax.experimental.pallas import tpu as pltpu
from jax.sharding import PartitionSpec as P

MESH = pl.DeviceIdType.MESH
PASSES = 2
CHUNK = 256
SLOTS = 16
WSLOTS = 8
DSLOTS = 8
LAG_SUM, LAG_HID, LAG_FWD, LAG_DOWN = 2, 5, 8, 10


def flip(b, r):
    out, k = b, 1
    while k <= r:
        if r & k:
            out = out + k * (1 - 2 * ((b // k) % 2))
        k *= 2
    return out


def kernel(n_loop, n_bulk, tok, gate_hbm, up_hbm, down_hbm, out,
           x, wg, wu, wd, part, core_rcv, ysum, y_rcv, hid, acc, out_snd, out_rcv,
           wg_sem, wu_sem, wd_sem, tok_send, tok_recv, core_send, core_recv,
           y_send, y_recv, hy_send, hy_recv, hc_send, hc_recv, out_send, out_recv):
    n_y = n_loop // 2
    rb, dl = tok.shape
    ff = gate_hbm.shape[1]
    dout = down_hbm.shape[1]
    steps = ff // CHUNK
    total = PASSES * steps
    per = n_bulk // PASSES
    rows = per * rb
    half = rows // 2
    r = half // n_y

    l = lax.axis_index("loop")
    b = lax.axis_index("bulk")
    y, c = l // 2, l % 2
    sib = y * 2 + (1 - c)
    oc = 1 - c

    def y_to(d):
        return lax.rem(y + d, n_y)

    def y_from(d):
        return lax.rem(y + n_y - d, n_y)

    def gu_copies(g):
        s = lax.rem(g, WSLOTS)
        col = pl.multiple_of(lax.rem(g, steps) * CHUNK, CHUNK)
        return (pltpu.make_async_copy(gate_hbm.at[:, pl.ds(col, CHUNK)], wg.at[s], wg_sem.at[s]),
                pltpu.make_async_copy(up_hbm.at[:, pl.ds(col, CHUNK)], wu.at[s], wu_sem.at[s]))

    def d_copy(g):
        s = lax.rem(g, DSLOTS)
        row = pl.multiple_of(lax.rem(g, steps) * CHUNK, CHUNK)
        return pltpu.make_async_copy(down_hbm.at[pl.ds(row, CHUNK), :], wd.at[s], wd_sem.at[s])

    for g in range(min(WSLOTS, total)):
        for cp in gu_copies(jnp.int32(g)):
            cp.start()
    for g in range(min(DSLOTS, total)):
        d_copy(jnp.int32(g)).start()

    barrier = pltpu.get_barrier_semaphore()
    pl.semaphore_signal(barrier, inc=1, device_id={"loop": sib}, device_id_type=MESH)
    for d in range(1, n_y):
        pl.semaphore_signal(barrier, inc=1, device_id={"loop": y_to(d) * 2 + c}, device_id_type=MESH)
    for q in range(1, n_bulk):
        pl.semaphore_signal(barrier, inc=1, device_id={"bulk": flip(b, q)}, device_id_type=MESH)
    pl.semaphore_wait(barrier, 1 + (n_y - 1) + (n_bulk - 1))

    def tok_copy(q):
        return pltpu.make_async_remote_copy(
            src_ref=tok, dst_ref=x.at[q], send_sem=tok_send.at[q], recv_sem=tok_recv.at[q],
            device_id={"bulk": flip(b, q)}, device_id_type=MESH)

    def core_copy(g):
        s = lax.rem(g, SLOTS)
        return pltpu.make_async_remote_copy(
            src_ref=part.at[s, oc], dst_ref=core_rcv.at[s], send_sem=core_send.at[s],
            recv_sem=core_recv.at[s], device_id={"loop": sib}, device_id_type=MESH)

    def y_copy(g, d):
        s = lax.rem(g, SLOTS)
        return pltpu.make_async_remote_copy(
            src_ref=ysum.at[s, y_to(d)], dst_ref=y_rcv.at[s, d - 1], send_sem=y_send.at[s, d - 1],
            recv_sem=y_recv.at[s, d - 1], device_id={"loop": y_to(d) * 2 + c}, device_id_type=MESH)

    def hy_copy(g, d):
        s = lax.rem(g, SLOTS)
        return pltpu.make_async_remote_copy(
            src_ref=hid.at[s, c, y], dst_ref=hid.at[s, c, y], send_sem=hy_send.at[s, d - 1],
            recv_sem=hy_recv.at[s, d - 1], device_id={"loop": y_to(d) * 2 + c}, device_id_type=MESH)

    def hy_wait(g, d):
        s = lax.rem(g, SLOTS)
        pltpu.make_async_remote_copy(
            src_ref=hid.at[s, c, y], dst_ref=hid.at[s, c, y_from(d)], send_sem=hy_send.at[s, d - 1],
            recv_sem=hy_recv.at[s, d - 1], device_id={"loop": y_to(d) * 2 + c},
            device_id_type=MESH).wait_recv()

    def hc_copy(g, d):
        s = lax.rem(g, SLOTS)
        return pltpu.make_async_remote_copy(
            src_ref=hid.at[s, c, y_from(d)], dst_ref=hid.at[s, c, y_from(d)], send_sem=hc_send.at[s, d],
            recv_sem=hc_recv.at[s, d], device_id={"loop": sib}, device_id_type=MESH)

    def hc_wait(g, d):
        s = lax.rem(g, SLOTS)
        pltpu.make_async_remote_copy(
            src_ref=hid.at[s, c, y_from(d)], dst_ref=hid.at[s, oc, y_from(d)], send_sem=hc_send.at[s, d],
            recv_sem=hc_recv.at[s, d], device_id={"loop": sib}, device_id_type=MESH).wait_recv()

    def out_copy(q):
        return pltpu.make_async_remote_copy(
            src_ref=out_snd.at[q], dst_ref=out_rcv.at[q], send_sem=out_send.at[q],
            recv_sem=out_recv.at[q], device_id={"bulk": flip(b, q)}, device_id_type=MESH)

    for q in range(1, per):
        tok_copy(q).start()
    x[0] = tok[...]
    acc[...] = jnp.zeros_like(acc)
    for q in range(1, per):
        tok_copy(q).wait_recv()
    for q in range(max(per, 1), n_bulk):
        tok_copy(q).start()

    def step(t, carry):
        @pl.when(t < total)
        def _():
            g = t
            p = g // steps
            s, w = lax.rem(g, SLOTS), lax.rem(g, WSLOTS)
            for pp in range(1, PASSES):
                @pl.when(g == pp * steps)
                def _():
                    for q in range(pp * per, (pp + 1) * per):
                        tok_copy(q).wait_recv()
            for cp in gu_copies(g):
                cp.wait()
            rows_x = x[pl.ds(p * per, per)].reshape(rows, dl)
            gp = jnp.dot(rows_x, wg[w], preferred_element_type=jnp.float32)
            part[s, :, :, :CHUNK] = gp.astype(jnp.bfloat16).reshape(2, half, CHUNK)
            up = jnp.dot(rows_x, wu[w], preferred_element_type=jnp.float32)
            part[s, :, :, CHUNK:] = up.astype(jnp.bfloat16).reshape(2, half, CHUNK)
            core_copy(g).start()

            @pl.when(g + WSLOTS < total)
            def _():
                for cp in gu_copies(g + WSLOTS):
                    cp.start()

        @pl.when((t >= LAG_SUM) & (t < total + LAG_SUM))
        def _():
            g = t - LAG_SUM
            s = lax.rem(g, SLOTS)
            core_copy(g).wait_recv()
            both = part[s, c].astype(jnp.float32) + core_rcv[s].astype(jnp.float32)
            ysum[s] = both.astype(jnp.bfloat16).reshape(n_y, r, 2 * CHUNK)
            for d in range(1, n_y):
                y_copy(g, d).start()

        @pl.when((t >= LAG_HID) & (t < total + LAG_HID))
        def _():
            g = t - LAG_HID
            s = lax.rem(g, SLOTS)
            tot = ysum[s, y].astype(jnp.float32)
            for d in range(1, n_y):
                y_copy(g, d).wait_recv()
                tot = tot + y_rcv[s, d - 1].astype(jnp.float32)
            gate, up = tot[:, :CHUNK], tot[:, CHUNK:]
            hid[s, c, y] = (gate / (1.0 + jnp.exp(-gate)) * up).astype(jnp.bfloat16)
            for d in range(1, n_y):
                hy_copy(g, d).start()
            hc_copy(g, 0).start()

        @pl.when((t >= LAG_FWD) & (t < total + LAG_FWD))
        def _():
            g = t - LAG_FWD
            for d in range(1, n_y):
                hy_wait(g, d)
                hc_copy(g, d).start()

        @pl.when(t >= LAG_DOWN)
        def _():
            g = t - LAG_DOWN
            p = g // steps
            s, w = lax.rem(g, SLOTS), lax.rem(g, DSLOTS)
            for d in range(n_y):
                hc_wait(g, d)
            d_copy(g).wait()
            acc[p] += jnp.dot(hid[s].reshape(rows, CHUNK), wd[w], preferred_element_type=jnp.float32)
            core_copy(g).wait_send()
            for d in range(1, n_y):
                y_copy(g, d).wait_send()
                hy_copy(g, d).wait_send()
            for d in range(n_y):
                hc_copy(g, d).wait_send()

            @pl.when(g + DSLOTS < total)
            def _():
                d_copy(g + DSLOTS).start()

            for pp in range(PASSES):
                @pl.when(g == pp * steps + steps - 1)
                def _():
                    for q in reversed(range(max(pp * per, 1), (pp + 1) * per)):
                        k = q - pp * per
                        out_snd[q] = acc[pp, k * rb:(k + 1) * rb].astype(jnp.bfloat16)
                        out_copy(q).start()
        return carry

    lax.fori_loop(0, total + LAG_DOWN, step, 0)

    res = acc[0, 0:rb]
    for q in range(1, n_bulk):
        out_copy(q).wait_recv()
        res = res + out_rcv[q].astype(jnp.float32)
    out[...] = res.astype(out.dtype)
    for q in range(1, n_bulk):
        tok_copy(q).wait_send()
        out_copy(q).wait_send()


def body(n_loop, n_bulk, tokens, gate_weight, up_weight, down_weight):
    rb, dl = tokens.shape
    ff, dout = down_weight.shape
    n_y = n_loop // 2
    rows = n_bulk // PASSES * rb
    half = rows // 2
    r = half // n_y
    bf, f32 = jnp.bfloat16, jnp.float32
    dma = pltpu.SemaphoreType.DMA
    vmem = pl.BlockSpec(memory_space=pltpu.VMEM)
    hbm = pl.BlockSpec(memory_space=pl.ANY)
    ny1 = max(n_y - 1, 1)
    return pl.pallas_call(
        functools.partial(kernel, n_loop, n_bulk),
        out_shape=jax.ShapeDtypeStruct((rb, dout), bf),
        in_specs=[vmem, hbm, hbm, hbm],
        out_specs=vmem,
        scratch_shapes=[
            pltpu.VMEM((n_bulk, rb, dl), bf),
            pltpu.VMEM((WSLOTS, dl, CHUNK), bf),
            pltpu.VMEM((WSLOTS, dl, CHUNK), bf),
            pltpu.VMEM((DSLOTS, CHUNK, dout), bf),
            pltpu.VMEM((SLOTS, 2, half, 2 * CHUNK), bf),
            pltpu.VMEM((SLOTS, half, 2 * CHUNK), bf),
            pltpu.VMEM((SLOTS, n_y, r, 2 * CHUNK), bf),
            pltpu.VMEM((SLOTS, ny1, r, 2 * CHUNK), bf),
            pltpu.VMEM((SLOTS, 2, n_y, r, CHUNK), bf),
            pltpu.VMEM((PASSES, rows, dout), f32),
            pltpu.VMEM((n_bulk, rb, dout), bf),
            pltpu.VMEM((n_bulk, rb, dout), bf),
            dma((WSLOTS,)), dma((WSLOTS,)), dma((DSLOTS,)),
            dma((n_bulk,)), dma((n_bulk,)),
            dma((SLOTS,)), dma((SLOTS,)),
            dma((SLOTS, ny1)), dma((SLOTS, ny1)),
            dma((SLOTS, ny1)), dma((SLOTS, ny1)),
            dma((SLOTS, n_y)), dma((SLOTS, n_y)),
            dma((n_bulk,)), dma((n_bulk,)),
        ],
        compiler_params=pltpu.CompilerParams(
            collective_id=0, has_side_effects=True, vmem_limit_bytes=58 * 1024 * 1024),
    )(tokens, gate_weight, up_weight, down_weight)


def solution(mesh):
    return jax.shard_map(
        functools.partial(body, mesh.shape["loop"], mesh.shape["bulk"]),
        mesh=mesh,
        in_specs=(
            P(("groups", "bulk"), "loop"),
            P("loop", "bulk"),
            P("loop", "bulk"),
            P("bulk", "loop"),
        ),
        out_specs=P(("groups", "bulk"), "loop"),
        check_vma=False,
    )
```

time: 215 us -> 104 us (0.48)
  waiting for transfers between devices: 152 us -> 0 us
  Pallas kernels: 0 us -> 102 us
  matrix products: 43.1 us -> 0 us
  between operations: 13.2 us -> 0.01 us
  other arithmetic: 6.73 us -> 0 us
    pallas_call x0 -> x1, Pallas kernels: none -> 102 us  [body(): pl.pallas_call(functools.partial(kernel, n_loop, n_bulk), out_shape=jax.S...]
    reduce_scatter x2 -> x0, waiting for transfers between devices: 88.7 us -> none  [the longest x1 61.5 us: body(): lax.psum_scatter(partial_sums.astype(jnp.bfloat16), 'loop', scatter_dimen...]
    all_gather x2 -> x0, waiting for transfers between devices: 62.4 us -> none  [the longest x1 32.3 us: body(): piece = lax.all_gather(tokens, 'bulk', axis=0, tiled=True)]
    dot_general x3 -> x0, matrix products: 43.1 us -> none  [the longest x1 16.4 us: body(): up_piece = jnp.dot(piece, up_weight, preferred_element_type=jnp.float32)]
    concatenate x1 -> x0, other arithmetic: 3.69 us -> none  [body(): partial_sums = jnp.concatenate([gate_piece, up_piece], axis=1)]
    convert_element_type x2 -> x0, other arithmetic: 3.04 us -> none  [the longest x1 1.67 us: body(): summed = lax.psum_scatter(partial_sums.astype(jnp.bfloat16), 'loop', scat...]
  transfers between devices with their start and end apart: 4 -> 0, of which waited for: 4 -> 0; matrix products, arithmetic and copies ran while one was open for 0% -> 0% of each run, Pallas kernels for 0% -> 0%
where the time goes in v1:
time: 104 us; the launch traced here: 103 us
  Pallas kernels  102 us (98%)
  local copies, waits for them, and re-layouts  1.67 us (2%)
    pallas_call x1, Pallas kernels, body(): pl.pallas_call(functools.partial(kernel, n_loop, n_bulk), out_shape=jax.S...  102 us

profile of v1, /device:TPU:0, one launch (start us, length us, event | category | flops | bytes accessed | tf_op | source)
XLA Modules:
  0.0 103.4 jit_solution(97967534299931571)
XLA Ops:
  0.0 101.7 %shard_map.46 = bf16[64,2048]{1,0:T(8,128)(2,1)} custom-call(bf16[64,2048]{1,0:T(8,128)(2,1)} %tok.1, bf16[2048,6656]{1,0:T(8,128)(2,1)} %gate_hbm.1, bf16[2048,6656]{1,0:T(8,128)(2,1)} %up_hbm.1, bf16[6656,2048]{1,0:T(8,128)(2,1)} %down_hbm.1), custom_call_target="tpu_custom_call" | custom-call | tf_op jit(solution)/shard_map/pallas_call | solution.py:245
  101.7 1.7 %copy.6 = bf16[64,2048]{1,0:T(8,128)(2,1)} copy(bf16[64,2048]{1,0:T(8,128)(2,1)} %shard_map.46) | data formatting | bytes 524288

commit v2 on v1

--- a/solution.py
+++ b/solution.py
@@ -9,11 +9,13 @@
 
 MESH = pl.DeviceIdType.MESH
 PASSES = 2
-CHUNK = 256
+CHUNK = 512
 SLOTS = 16
-WSLOTS = 8
-DSLOTS = 8
-LAG_SUM, LAG_HID, LAG_FWD, LAG_DOWN = 2, 5, 8, 10
+WSLOTS = 4
+DSLOTS = 4
+PIECES = 4
+LAGS = (1, 4, 7, 8)
+LAG_SUM, LAG_HID, LAG_FWD, LAG_DOWN = LAGS
 
 
 def flip(b, r):
@@ -26,13 +28,14 @@
 
 
 def kernel(n_loop, n_bulk, tok, gate_hbm, up_hbm, down_hbm, out,
-           x, wg, wu, wd, part, core_rcv, ysum, y_rcv, hid, acc, out_snd, out_rcv,
+           x, wg, wu, wd, part, core_rcv, ysum, y_rcv, hid, acc, out_snd, out_mid, out_rcv,
            wg_sem, wu_sem, wd_sem, tok_send, tok_recv, core_send, core_recv,
-           y_send, y_recv, hy_send, hy_recv, hc_send, hc_recv, out_send, out_recv):
+           y_send, y_recv, hy_send, hy_recv, hc_send, hc_recv, mid_send, mid_recv, out_send, out_recv):
     n_y = n_loop // 2
     rb, dl = tok.shape
     ff = gate_hbm.shape[1]
     dout = down_hbm.shape[1]
+    wp = dout // PIECES
     steps = ff // CHUNK
     total = PASSES * steps
     per = n_bulk // PASSES
@@ -119,10 +122,15 @@
             src_ref=hid.at[s, c, y_from(d)], dst_ref=hid.at[s, oc, y_from(d)], send_sem=hc_send.at[s, d],
             recv_sem=hc_recv.at[s, d], device_id={"loop": sib}, device_id_type=MESH).wait_recv()
 
-    def out_copy(q):
-        return pltpu.make_async_remote_copy(
-            src_ref=out_snd.at[q], dst_ref=out_rcv.at[q], send_sem=out_send.at[q],
-            recv_sem=out_recv.at[q], device_id={"bulk": flip(b, q)}, device_id_type=MESH)
+    def mid_copy(q, k):
+        return pltpu.make_async_remote_copy(
+            src_ref=out_snd.at[q, k], dst_ref=out_mid.at[q // 2, k], send_sem=mid_send.at[q // 2, k],
+            recv_sem=mid_recv.at[q // 2, k], device_id={"bulk": flip(b, 1)}, device_id_type=MESH)
+
+    def out_copy(q, k):
+        return pltpu.make_async_remote_copy(
+            src_ref=out_snd.at[q, k], dst_ref=out_rcv.at[q // 2, k], send_sem=out_send.at[q // 2, k],
+            recv_sem=out_recv.at[q // 2, k], device_id={"bulk": flip(b, q)}, device_id_type=MESH)
 
     for q in range(1, per):
         tok_copy(q).start()
@@ -212,22 +220,38 @@
             for pp in range(PASSES):
                 @pl.when(g == pp * steps + steps - 1)
                 def _():
-                    for q in reversed(range(max(pp * per, 1), (pp + 1) * per)):
-                        k = q - pp * per
-                        out_snd[q] = acc[pp, k * rb:(k + 1) * rb].astype(jnp.bfloat16)
-                        out_copy(q).start()
+                    evens = range(pp * per, (pp + 1) * per, 2)
+                    for k in range(PIECES):
+                        for q in evens:
+                            m = (q + 1 - pp * per) * rb
+                            out_snd[q + 1, k] = acc[pp, m:m + rb, k * wp:(k + 1) * wp].astype(jnp.bfloat16)
+                            mid_copy(q + 1, k).start()
+                    for k in range(PIECES):
+                        for q in evens:
+                            if q:
+                                m = (q - pp * per) * rb
+                                mid_copy(q + 1, k).wait_recv()
+                                out_snd[q, k] = (acc[pp, m:m + rb, k * wp:(k + 1) * wp]
+                                                 + out_mid[q // 2, k].astype(jnp.float32)).astype(jnp.bfloat16)
+                                out_copy(q, k).start()
         return carry
 
     lax.fori_loop(0, total + LAG_DOWN, step, 0)
 
-    res = acc[0, 0:rb]
-    for q in range(1, n_bulk):
-        out_copy(q).wait_recv()
-        res = res + out_rcv[q].astype(jnp.float32)
-    out[...] = res.astype(out.dtype)
+    for k in range(PIECES):
+        mid_copy(1, k).wait_recv()
+        res = acc[0, 0:rb, k * wp:(k + 1) * wp] + out_mid[0, k].astype(jnp.float32)
+        for q in range(2, n_bulk, 2):
+            out_copy(q, k).wait_recv()
+            res = res + out_rcv[q // 2, k].astype(jnp.float32)
+        out[:, k * wp:(k + 1) * wp] = res.astype(out.dtype)
     for q in range(1, n_bulk):
         tok_copy(q).wait_send()
-        out_copy(q).wait_send()
+    for k in range(PIECES):
+        for q in range(0, n_bulk, 2):
+            mid_copy(q + 1, k).wait_send()
+            if q:
+                out_copy(q, k).wait_send()
 
 
 def body(n_loop, n_bulk, tokens, gate_weight, up_weight, down_weight):
@@ -258,15 +282,17 @@
             pltpu.VMEM((SLOTS, ny1, r, 2 * CHUNK), bf),
             pltpu.VMEM((SLOTS, 2, n_y, r, CHUNK), bf),
             pltpu.VMEM((PASSES, rows, dout), f32),
-            pltpu.VMEM((n_bulk, rb, dout), bf),
-            pltpu.VMEM((n_bulk, rb, dout), bf),
+            pltpu.VMEM((n_bulk, PIECES, rb, dout // PIECES), bf),
+            pltpu.VMEM((n_bulk // 2, PIECES, rb, dout // PIECES), bf),
+            pltpu.VMEM((n_bulk // 2, PIECES, rb, dout // PIECES), bf),
             dma((WSLOTS,)), dma((WSLOTS,)), dma((DSLOTS,)),
             dma((n_bulk,)), dma((n_bulk,)),
             dma((SLOTS,)), dma((SLOTS,)),
             dma((SLOTS, ny1)), dma((SLOTS, ny1)),
             dma((SLOTS, ny1)), dma((SLOTS, ny1)),
             dma((SLOTS, n_y)), dma((SLOTS, n_y)),
-            dma((n_bulk,)), dma((n_bulk,)),
+            dma((n_bulk // 2, PIECES)), dma((n_bulk // 2, PIECES)),
+            dma((n_bulk // 2, PIECES)), dma((n_bulk // 2, PIECES)),
         ],
         compiler_params=pltpu.CompilerParams(
             collective_id=0, has_side_effects=True, vmem_limit_bytes=58 * 1024 * 1024),

time: 104 us -> 94.7 us (0.911)
  Pallas kernels: 102 us -> 92.8 us
    pallas_call x1, Pallas kernels: 102 us -> 92.8 us  [body(): pl.pallas_call(functools.partial(kernel, n_loop, n_bulk), out_shape=jax.S...]
where the time goes in v2:
time: 94.7 us; the launch traced here: 94.5 us
  Pallas kernels  92.8 us (98%)
  local copies, waits for them, and re-layouts  1.67 us (2%)
    pallas_call x1, Pallas kernels, body(): pl.pallas_call(functools.partial(kernel, n_loop, n_bulk), out_shape=jax.S...  92.8 us

profile of v2, /device:TPU:0, one launch (start us, length us, event | category | flops | bytes accessed | tf_op | source)
XLA Modules:
  0.0 94.5 jit_solution(16310957991033839669)
XLA Ops:
  0.0 92.8 %shard_map.46 = bf16[64,2048]{1,0:T(8,128)(2,1)} custom-call(bf16[64,2048]{1,0:T(8,128)(2,1)} %tok.1, bf16[2048,6656]{1,0:T(8,128)(2,1)} %gate_hbm.1, bf16[2048,6656]{1,0:T(8,128)(2,1)} %up_hbm.1, bf16[6656,2048]{1,0:T(8,128)(2,1)} %down_hbm.1), custom_call_target="tpu_custom_call" | custom-call | tf_op jit(solution)/shard_map/pallas_call | solution.py:269
  92.8 1.7 %copy.6 = bf16[64,2048]{1,0:T(8,128)(2,1)} copy(bf16[64,2048]{1,0:T(8,128)(2,1)} %shard_map.46) | data formatting | bytes 524288

commit v3 on v2

--- a/solution.py
+++ b/solution.py
@@ -9,13 +9,17 @@
 
 MESH = pl.DeviceIdType.MESH
 PASSES = 2
-CHUNK = 512
+CHUNKS = (512, 256, 128)
 SLOTS = 16
 WSLOTS = 4
 DSLOTS = 4
 PIECES = 4
 LAGS = (1, 4, 7, 8)
 LAG_SUM, LAG_HID, LAG_FWD, LAG_DOWN = LAGS
+
+
+def width(ff):
+    return next(c for c in CHUNKS if ff % c == 0)
 
 
 def flip(b, r):
@@ -34,9 +38,10 @@
     n_y = n_loop // 2
     rb, dl = tok.shape
     ff = gate_hbm.shape[1]
+    chunk = width(ff)
     dout = down_hbm.shape[1]
     wp = dout // PIECES
-    steps = ff // CHUNK
+    steps = ff // chunk
     total = PASSES * steps
     per = n_bulk // PASSES
     rows = per * rb
@@ -57,14 +62,14 @@
 
     def gu_copies(g):
         s = lax.rem(g, WSLOTS)
-        col = pl.multiple_of(lax.rem(g, steps) * CHUNK, CHUNK)
-        return (pltpu.make_async_copy(gate_hbm.at[:, pl.ds(col, CHUNK)], wg.at[s], wg_sem.at[s]),
-                pltpu.make_async_copy(up_hbm.at[:, pl.ds(col, CHUNK)], wu.at[s], wu_sem.at[s]))
+        col = pl.multiple_of(lax.rem(g, steps) * chunk, chunk)
+        return (pltpu.make_async_copy(gate_hbm.at[:, pl.ds(col, chunk)], wg.at[s], wg_sem.at[s]),
+                pltpu.make_async_copy(up_hbm.at[:, pl.ds(col, chunk)], wu.at[s], wu_sem.at[s]))
 
     def d_copy(g):
         s = lax.rem(g, DSLOTS)
-        row = pl.multiple_of(lax.rem(g, steps) * CHUNK, CHUNK)
-        return pltpu.make_async_copy(down_hbm.at[pl.ds(row, CHUNK), :], wd.at[s], wd_sem.at[s])
+        row = pl.multiple_of(lax.rem(g, steps) * chunk, chunk)
+        return pltpu.make_async_copy(down_hbm.at[pl.ds(row, chunk), :], wd.at[s], wd_sem.at[s])
 
     for g in range(min(WSLOTS, total)):
         for cp in gu_copies(jnp.int32(g)):
@@ -156,9 +161,9 @@
                 cp.wait()
             rows_x = x[pl.ds(p * per, per)].reshape(rows, dl)
             gp = jnp.dot(rows_x, wg[w], preferred_element_type=jnp.float32)
-            part[s, :, :, :CHUNK] = gp.astype(jnp.bfloat16).reshape(2, half, CHUNK)
+            part[s, :, :, :chunk] = gp.astype(jnp.bfloat16).reshape(2, half, chunk)
             up = jnp.dot(rows_x, wu[w], preferred_element_type=jnp.float32)
-            part[s, :, :, CHUNK:] = up.astype(jnp.bfloat16).reshape(2, half, CHUNK)
+            part[s, :, :, chunk:] = up.astype(jnp.bfloat16).reshape(2, half, chunk)
             core_copy(g).start()
 
             @pl.when(g + WSLOTS < total)
@@ -172,7 +177,7 @@
             s = lax.rem(g, SLOTS)
             core_copy(g).wait_recv()
             both = part[s, c].astype(jnp.float32) + core_rcv[s].astype(jnp.float32)
-            ysum[s] = both.astype(jnp.bfloat16).reshape(n_y, r, 2 * CHUNK)
+            ysum[s] = both.astype(jnp.bfloat16).reshape(n_y, r, 2 * chunk)
             for d in range(1, n_y):
                 y_copy(g, d).start()
 
@@ -184,7 +189,7 @@
             for d in range(1, n_y):
                 y_copy(g, d).wait_recv()
                 tot = tot + y_rcv[s, d - 1].astype(jnp.float32)
-            gate, up = tot[:, :CHUNK], tot[:, CHUNK:]
+            gate, up = tot[:, :chunk], tot[:, chunk:]
             hid[s, c, y] = (gate / (1.0 + jnp.exp(-gate)) * up).astype(jnp.bfloat16)
             for d in range(1, n_y):
                 hy_copy(g, d).start()
@@ -205,7 +210,7 @@
             for d in range(n_y):
                 hc_wait(g, d)
             d_copy(g).wait()
-            acc[p] += jnp.dot(hid[s].reshape(rows, CHUNK), wd[w], preferred_element_type=jnp.float32)
+            acc[p] += jnp.dot(hid[s].reshape(rows, chunk), wd[w], preferred_element_type=jnp.float32)
             core_copy(g).wait_send()
             for d in range(1, n_y):
                 y_copy(g, d).wait_send()
@@ -257,6 +262,7 @@
 def body(n_loop, n_bulk, tokens, gate_weight, up_weight, down_weight):
     rb, dl = tokens.shape
     ff, dout = down_weight.shape
+    chunk = width(ff)
     n_y = n_loop // 2
     rows = n_bulk // PASSES * rb
     half = rows // 2
@@ -273,14 +279,14 @@
         out_specs=vmem,
         scratch_shapes=[
             pltpu.VMEM((n_bulk, rb, dl), bf),
-            pltpu.VMEM((WSLOTS, dl, CHUNK), bf),
-            pltpu.VMEM((WSLOTS, dl, CHUNK), bf),
-            pltpu.VMEM((DSLOTS, CHUNK, dout), bf),
-            pltpu.VMEM((SLOTS, 2, half, 2 * CHUNK), bf),
-            pltpu.VMEM((SLOTS, half, 2 * CHUNK), bf),
-            pltpu.VMEM((SLOTS, n_y, r, 2 * CHUNK), bf),
-            pltpu.VMEM((SLOTS, ny1, r, 2 * CHUNK), bf),
-            pltpu.VMEM((SLOTS, 2, n_y, r, CHUNK), bf),
+            pltpu.VMEM((WSLOTS, dl, chunk), bf),
+            pltpu.VMEM((WSLOTS, dl, chunk), bf),
+            pltpu.VMEM((DSLOTS, chunk, dout), bf),
+            pltpu.VMEM((SLOTS, 2, half, 2 * chunk), bf),
+            pltpu.VMEM((SLOTS, half, 2 * chunk), bf),
+            pltpu.VMEM((SLOTS, n_y, r, 2 * chunk), bf),
+            pltpu.VMEM((SLOTS, ny1, r, 2 * chunk), bf),
+            pltpu.VMEM((SLOTS, 2, n_y, r, chunk), bf),
             pltpu.VMEM((PASSES, rows, dout), f32),
             pltpu.VMEM((n_bulk, PIECES, rb, dout // PIECES), bf),
             pltpu.VMEM((n_bulk // 2, PIECES, rb, dout // PIECES), bf),

time: 94.7 us -> 94.7 us (level)
  no operation moved by 1% of the time
where the time goes in v3:
time: 94.7 us; the launch traced here: 94.5 us
  Pallas kernels  92.8 us (98%)
  local copies, waits for them, and re-layouts  1.67 us (2%)
    pallas_call x1, Pallas kernels, body(): pl.pallas_call(functools.partial(kernel, n_loop, n_bulk), out_shape=jax.S...  92.8 us

profile of v3, /device:TPU:0, one launch (start us, length us, event | category | flops | bytes accessed | tf_op | source)
XLA Modules:
  0.0 94.5 jit_solution(16310957991033839669)
XLA Ops:
  0.0 92.8 %shard_map.46 = bf16[64,2048]{1,0:T(8,128)(2,1)} custom-call(bf16[64,2048]{1,0:T(8,128)(2,1)} %tok.1, bf16[2048,6656]{1,0:T(8,128)(2,1)} %gate_hbm.1, bf16[2048,6656]{1,0:T(8,128)(2,1)} %up_hbm.1, bf16[6656,2048]{1,0:T(8,128)(2,1)} %down_hbm.1), custom_call_target="tpu_custom_call" | custom-call | tf_op jit(solution)/shard_map/pallas_call | solution.py:275
  92.8 1.7 %copy.6 = bf16[64,2048]{1,0:T(8,128)(2,1)} copy(bf16[64,2048]{1,0:T(8,128)(2,1)} %shard_map.46) | data formatting | bytes 524288
